TPU v7x, 32 devices: a whole 2x2x4 slice. The times are simulated.
32 devices in a mesh: grp: 4 (over z), dev: 8 (over y, x, core).
Axes of the slice: x: 2, y: 2, z: 4, core: 2. Of those that a mesh axis runs over, the one named last changes fastest.
Arguments:
- orbitals: bfloat16 [64, 48, 2304], P(('grp', 'dev')), may hold values from -6 to 6
- offsets: int32 [64, 3], P(('grp', 'dev')), may hold values from 0 to 23
- pick: int32 [4, 8, 4], P('grp'), may hold values from 0 to 1
- pair_local: int32 [4, 8, 2], P('grp', 'dev'), may hold values from 0 to 1
- pair_source: int32 [4, 8, 2], P('grp', 'dev'), may hold values from 0 to 3, as said below
- pair_count: int32 [4, 8, 1], P('grp', 'dev'), may hold values from 1 to 2, as said below
Outputs:
- exchange_action: float32 [64, 110592], P('grp', 'dev')
Inputs may be any that keep to these rules, and one draw needn't show every extreme that they name: pair_source[g, d, p] is never g; the two slots of one device's list name different groups. Only the first pair_count[g, d, 0] slots of a device's lists are pairs; some device lists exactly 2.
All inputs are finite; a program needn't handle non-finite values.
Results may differ from a plain program's by a relative error of at most 0.002.
Values may be sent and summed in bfloat16 or wider, within the bound.
No kernel may reach another device: no remote copies, remote signals or barrier semaphores. Data moves between devices by JAX's collectives and lax.ppermute only.
A program may use at most 64 MiB of HBM per device.

v0:
```python
import functools
import math

import numpy as np

import jax
import jax.numpy as jnp
from jax import lax
from jax.experimental import pallas as pl
from jax.experimental.pallas import tpu as pltpu
from jax.sharding import PartitionSpec as P

LANES = 128
HALF = 64
ROWS = 16
f32 = jnp.float32
bf16 = jnp.bfloat16


def np_tables(n):
    freq = np.arange(n)
    step = math.pi / (n + 1)
    sine = math.sqrt(2.0 / (n + 1)) * np.sin(step * ((freq[:, None] + 1) * (freq[None, :] + 1) % (2 * (n + 1))))
    sine = sine.astype(np.float32)
    high = sine.astype(jnp.bfloat16)
    low = (sine - high.astype(np.float32)).astype(jnp.bfloat16)

    def two(block):
        out = np.zeros((LANES, LANES), jnp.bfloat16)
        out[:n, :n] = block
        out[HALF : HALF + n, HALF : HALF + n] = block
        return out

    lane_side = np.block([[two(high), two(low)], [two(high), two(low)]])
    row_side = np.concatenate([high, high, low, 0 * low], axis=1)
    modes = (2.0 - 2.0 * np.cos(step * (freq + 1.0))).astype(np.float32)
    base = np.ones((n, LANES), np.float32)
    outer = np.ones((n // 2, LANES), np.float32)
    for half in range(2):
        at = half * HALF
        base[:, at : at + n] = modes[:, None] + modes[None, :]
        outer[:, at : at + HALF] = modes[half * (n // 2) : (half + 1) * (n // 2), None]
    pad = np.zeros((n, 2 * LANES - 4 * n), jnp.bfloat16)
    sines = np.concatenate([lane_side, np.concatenate([row_side, pad], axis=1)]).astype(np.float32)
    modes = np.concatenate([base, outer])
    modes = np.pad(modes, ((0, len(sines) - len(modes)), (0, 0)))
    return np.concatenate([sines, modes], axis=1)


def split(x):
    high = x.astype(bf16)
    return high, (x - high.astype(f32)).astype(bf16)


def lane_turn(x, lane_side):
    both = jnp.concatenate(split(x), axis=1)
    out = jnp.dot(both, lane_side, preferred_element_type=f32)
    return out[:, :LANES] + out[:, LANES:]


def row_turn(tiles, row_side):
    columns = []
    for tile in tiles:
        high, low = split(tile)
        columns.append(jnp.concatenate([high, low, high], axis=0))
    out = jnp.dot(row_side, jnp.concatenate(columns, axis=1), preferred_element_type=f32)
    return [out[:, k * LANES : (k + 1) * LANES] for k in range(len(tiles))]


def unpack(dense, put):
    n = dense.shape[0]
    half = n // 2
    lane = lax.broadcasted_iota(jnp.int32, (n, LANES), 1)
    for yo in range(half):
        start = yo * n % LANES
        halves = []
        for h in range(2):
            t = (yo * n // LANES + h * (half * n // LANES)) * LANES
            piece = dense[:, t : t + LANES].astype(f32)
            if start + n > LANES:
                after = dense[:, t + LANES : t + 2 * LANES].astype(f32)
                piece = jnp.where(lane >= start, piece, after)
            amount = (h * HALF - start) % LANES
            halves.append(pltpu.roll(piece, amount, 1) if amount else piece)
        put(yo, jnp.where(lane < HALF, halves[0], halves[1]))


def setup_kernel(own, table, mine, held, sines, modes, total):
    orbs, n, _ = own.shape
    half = n // 2
    wide = n + 2 * half
    for q in range(orbs):

        def put(yo, tile, q=q):
            at = (q * half + yo) * wide + half
            held[at : at + n, :] = tile

        unpack(own.at[q], put)
    sines[...] = table[:, : 2 * LANES].astype(bf16)
    modes[...] = table[: modes.shape[0], 2 * LANES :]
    total[...] = jnp.zeros_like(total)


def pair_kernel(sizes, pieces, tasks, last, *refs):
    n, orbs, slots = sizes
    half = n // 2
    cells_tile = half * n // LANES
    wide = n + 2 * half
    mine, own, sines, modes = refs[:4]
    others = refs[4 : 4 + orbs]
    total_in = refs[4 + orbs]
    rest = list(refs[5 + orbs :])
    if last:
        outs = [rest.pop(0) for _ in range(max(pieces, 1))]
        total = rest.pop(0)
        flat = rest.pop(0) if pieces else None
    else:
        total = rest.pop(0)
    dense, held, moved, field, other, theirs = rest
    lists = others[-1][:, n * n * n // ROWS :].astype(f32).astype(jnp.int32)
    for k in range(mine.shape[1]):
        theirs[0, k] = lists[0, k]

    def fetch(q):
        if q < orbs - 1:
            dense[...] = others[q][...]
        else:
            for r in range(n // ROWS):
                dense[r * ROWS : (r + 1) * ROWS, :] = others[q][:, r * n * n : (r + 1) * n * n]

    lane = lax.broadcasted_iota(jnp.int32, (n, LANES), 1)
    row = lax.broadcasted_iota(jnp.int32, (n, LANES), 0)
    left_half = lane[:half] < HALF
    total[...] = total_in[...]

    at_source = 3 * orbs + slots
    at_count = at_source + slots
    at_group = at_count + 1
    at_pick = at_group + 2
    member = mine[0, at_group + 1]

    def tile_at(base, yo):
        return pl.ds(base + yo * wide + half, n)

    def shifted(ref, base, gap, use):
        gap_x, gap_y, gap_z = gap
        z_at = lax.rem(lane, HALF)
        inside = (
            (z_at < n)
            & (z_at + gap_z >= 0)
            & (z_at + gap_z < n)
            & (row + gap_x >= 0)
            & (row + gap_x < n)
        )
        for yo in range(half):
            s = gap_y + yo
            under = s < 0
            over = s >= half
            src = s + jnp.where(under, half, 0) - jnp.where(over, half, 0)
            tile = ref[pl.ds(base + src * wide + half + gap_x, n), :]
            amount = (2 * LANES - gap_z + jnp.where(under | over, HALF, 0)) % LANES
            tile = pltpu.roll(tile, amount, 1)
            low_lane = jnp.where(under, HALF, 0)
            high_lane = jnp.where(over, HALF, LANES)
            good = inside & (lane >= low_lane) & (lane < high_lane)
            use(yo, jnp.where(good, tile, 0.0))

    def swapped(ref, at):
        a = ref[pl.ds(at, half, stride=n), :]
        b = ref[pl.ds(at + half, half, stride=n), :]
        top = jnp.where(left_half, a, pltpu.roll(b, HALF, 1))
        bottom = jnp.where(left_half, pltpu.roll(a, HALF, 1), b)
        return jnp.concatenate([top, bottom], axis=0)

    def rows_of(ref, at):
        return ref[at * n : (at + 1) * n, :]

    def task(outgoing):
        lister, source = (mine, theirs) if outgoing else (theirs, mine)
        source_group = source[0, at_group]
        listed = lister[0, at_count]
        i_at = jnp.int32(0)
        found = jnp.int32(0)
        for p in range(slots):
            hit = (lister[0, at_source + p] == source_group) & (p < listed)
            i_at = jnp.where(hit, lister[0, 3 * orbs + p], i_at)
            found = jnp.where(hit, 1, found)
        j_at = source[0, at_pick + lister[0, at_group]]
        gap = [lister[0, i_at * 3 + k] - source[0, j_at * 3 + k] for k in range(3)]
        own_at, other_at = (i_at, j_at) if outgoing else (j_at, i_at)
        base = own_at * (half * wide)
        box_i, base_i, box_j, base_j = (own, base, held, 0) if outgoing else (held, 0, own, base)

        @pl.when(found == 1)
        def _():
            for q in range(orbs):
                @pl.when(other_at == q)
                def _():
                    fetch(q)

            def put(yo, tile):
                held[tile_at(0, yo), :] = tile

            unpack(dense, put)

            def use_moved(yo, tile):
                moved[yo * n : (yo + 1) * n, :] = tile
                field[yo * n : (yo + 1) * n, :] = box_i[tile_at(base_i, yo), :] * tile

            shifted(box_j, base_j, gap, use_moved)
            lane_side = sines[: 2 * LANES, :]
            row_side = sines[2 * LANES :, : 3 * n]
            other[...] = lane_turn(field[...], lane_side)
            tiles = row_turn([rows_of(other, at) for at in range(half)], row_side)
            for at in range(half):
                field[at * n : (at + 1) * n, :] = tiles[at]
            tiles = row_turn([swapped(field, at) for at in range(half)], row_side)
            tiles = [tiles[at] / (modes[:n, :] + modes[n + at : n + at + 1, :]) for at in range(half)]
            tiles = row_turn(tiles, row_side)
            for at in range(half):
                other[at * n : (at + 1) * n, :] = tiles[at]
            tiles = row_turn([swapped(other, at) for at in range(half)], row_side)
            for at in range(half):
                field[at * n : (at + 1) * n, :] = tiles[at]
            field[...] = lane_turn(field[...], lane_side)

            if outgoing:
                for yo in range(half):
                    there = pl.ds(own_at * (half * n) + yo * n, n)
                    total[there, :] += rows_of(field, yo) * rows_of(moved, yo)
            else:
                for yo in range(half):
                    term = rows_of(field, yo) * held[tile_at(0, yo), :]
                    held[tile_at(0, yo), :] = term.astype(bf16).astype(f32)

                def add_back(yo, tile):
                    there = pl.ds(own_at * (half * n) + yo * n, n)
                    total[there, :] += tile

                shifted(held, 0, [-k for k in gap], add_back)

    for outgoing in tasks:
        task(outgoing)

    if last:
        for a in range(orbs):
            current = {}
            for yo in range(half):
                start = yo * n % LANES
                first_tile = yo * n // LANES
                tile = total[a * half * n + yo * n : a * half * n + (yo + 1) * n, :]
                for h in range(2):
                    t = first_tile + h * cells_tile
                    amount = (start - h * HALF) % LANES
                    piece = pltpu.roll(tile, amount, 1) if amount else tile
                    current[t] = jnp.where(lane >= start, piece, current[t]) if t in current else piece
                    if start + n >= LANES:
                        here = slice(t * LANES, (t + 1) * LANES)
                        if pieces:
                            flat[pl.ds(t * orbs * n + a, n, stride=orbs), :] = current.pop(t)
                        else:
                            outs[0][a, :, here] = current.pop(t).astype(bf16)
                        if start + n > LANES:
                            current[t + 1] = piece
        depth = n // pieces * orbs if pieces else 0
        tiles = n * n // LANES
        for k in range(pieces):
            at = jnp.bitwise_xor(member, k) * depth
            for t in range(tiles):
                outs[k][:, t * LANES : (t + 1) * LANES] = flat[pl.ds(t * orbs * n + at, 8), :].astype(bf16)
            for t in range(tiles // 2):
                tail = [flat[pl.ds((t + h * tiles // 2) * orbs * n + at + 8, 4), :] for h in range(2)]
                tail_at = (tiles + t) * LANES
                outs[k][:, tail_at : tail_at + LANES] = jnp.concatenate(tail, axis=0).astype(bf16)


def pack_kernel(groups, offsets, pick, pair_local, pair_source, pair_count, orbitals, *outs):
    box, mine = outs
    _, n, plane = orbitals.shape
    orbs = offsets.shape[0]
    group = lax.axis_index("grp").astype(jnp.int32)
    member = lax.axis_index("dev").astype(jnp.int32)
    slots = pair_local.shape[2]
    numbers = [offsets[a, k] for a in range(orbs) for k in range(3)]
    numbers += [pair_local[0, 0, p] for p in range(slots)]
    numbers += [pair_source[0, 0, p] for p in range(slots)]
    numbers += [pair_count[0, 0, 0], group, member]
    numbers += [pick[0, g, member] for g in range(groups)]
    lane = lax.broadcasted_iota(jnp.int32, (ROWS, LANES), 1)
    row = jnp.zeros((ROWS, LANES), jnp.int32)
    for k, number in enumerate(numbers):
        mine[0, k] = number
        row = jnp.where(lane == k, number, row)
    for r in range(n // ROWS):
        box[:, r * plane : (r + 1) * plane] = orbitals[0, r * ROWS : (r + 1) * ROWS, :]
    box[:, n * plane // ROWS :] = row.astype(f32).astype(bf16)


def setup(own, table, mine):
    orbs, n, _ = own.shape
    half = n // 2
    vmem = pl.BlockSpec(memory_space=pltpu.VMEM)
    return pl.pallas_call(
        setup_kernel,
        out_shape=[
            jax.ShapeDtypeStruct((orbs * half * (n + 2 * half), LANES), f32),
            jax.ShapeDtypeStruct((table.shape[0], 2 * LANES), bf16),
            jax.ShapeDtypeStruct((n + half, LANES), f32),
            jax.ShapeDtypeStruct((orbs * half * n, LANES), f32),
        ],
        in_specs=[vmem, vmem, pl.BlockSpec(memory_space=pltpu.SMEM)],
        out_specs=[vmem] * 4,
        compiler_params=pltpu.CompilerParams(vmem_limit_bytes=16 << 20),
        name="setup",
    )(own, table, mine)


def pair_step(name, n, slots, pieces, tasks, last, mine, own, sines, modes, others, total):
    orbs = len(others)
    plane = n * n
    half = n // 2
    pieces = pieces if last else 0
    vmem = pl.BlockSpec(memory_space=pltpu.VMEM)
    smem = pl.BlockSpec(memory_space=pltpu.SMEM)
    held = jax.ShapeDtypeStruct(total.shape, f32)
    rows = half * n
    scratch = [
        pltpu.VMEM((n, plane), bf16),
        pltpu.VMEM((half * (n + 2 * half), LANES), f32),
        pltpu.VMEM((rows, LANES), f32),
        pltpu.VMEM((rows, LANES), f32),
        pltpu.VMEM((rows, LANES), f32),
        pltpu.SMEM(mine.shape, jnp.int32),
    ]
    shapes = held
    if last:
        shapes = jax.ShapeDtypeStruct((orbs, n, plane), bf16)
        if pieces:
            scratch.insert(0, pltpu.VMEM((orbs * n * plane // LANES + 8, LANES), f32))
            shapes = [jax.ShapeDtypeStruct((8, orbs * n * plane // pieces // 8), bf16)] * pieces
        scratch.insert(0, pltpu.VMEM(held.shape, f32))
    return pl.pallas_call(
        functools.partial(pair_kernel, (n, orbs, slots), pieces, tasks, last),
        out_shape=shapes,
        in_specs=[smem] + [vmem] * (4 + orbs),
        out_specs=[vmem] * pieces if pieces else vmem,
        scratch_shapes=scratch,
        input_output_aliases={} if last else {4 + orbs: 0},
        compiler_params=pltpu.CompilerParams(vmem_limit_bytes=32 << 20),
        cost_estimate=pl.CostEstimate(flops=2 * 12 * 3 * n**4, bytes_accessed=4 * n**3 * 4, transcendentals=0),
        name=name,
    )(mine, own, sines, modes, *others, total)


def gather_kernel(n, orbs, member_ref, *refs):
    devices = len(refs) - 3
    out, rows, mixed = refs[devices:]
    tiles = n * n // LANES
    member = member_ref[0]
    for k in range(devices):
        at = pl.multiple_of(jnp.bitwise_xor(member, k) * 8, 8)
        for t in range(tiles * 3 // 2):
            rows[pl.ds(t * devices * 8 + at, 8), :] = refs[k][:, t * LANES : (t + 1) * LANES].astype(f32)
    for x in range(n // devices):
        for t in range(tiles):
            here = slice((x * tiles + t) * LANES, (x * tiles + t + 1) * LANES)
            at = (x * tiles + t) * orbs * devices
            for a in range(orbs):
                q = x * orbs + a
                tile = t
                if q >= 8:
                    q += 4 * (t * 2 // tiles) - 8
                    tile = tiles + t % (tiles // 2)
                mixed[pl.ds(at + a, devices, stride=orbs), :] = rows[
                    pl.ds(tile * devices * 8 + q, devices, stride=8), :
                ]
            out[:, here] = mixed[at : at + orbs * devices, :]


def body(orbitals, offsets, pick, pair_local, pair_source, pair_count):
    orbs, n, plane = orbitals.shape
    groups = lax.axis_size("grp")
    devices = lax.axis_size("dev")
    member = lax.axis_index("dev").astype(jnp.int32)
    slots = pair_local.shape[2]
    vmem = pl.BlockSpec(memory_space=pltpu.VMEM)
    smem = pl.BlockSpec(memory_space=pltpu.SMEM)
    table = jnp.asarray(np_tables(n))
    numbers = 3 * orbs + 2 * slots + 3 + groups
    last_box, mine = pl.pallas_call(
        functools.partial(pack_kernel, groups),
        grid=(1,),
        out_shape=[
            jax.ShapeDtypeStruct((ROWS, n * plane // ROWS + LANES), bf16),
            jax.ShapeDtypeStruct((1, numbers), jnp.int32),
        ],
        in_specs=[smem] * 4 + [vmem, pl.BlockSpec((1, n, plane), lambda i: (orbs - 1, 0, 0))],
        out_specs=[vmem, smem],
        name="pack",
    )(offsets, pick.transpose(0, 2, 1), pair_local, pair_source, pair_count, orbitals)
    held = [orbitals[q] for q in range(orbs - 1)] + [last_box]
    by_pieces = devices & (devices - 1) == 0 and n % devices == 0 and n // devices * orbs == 12
    pieces = devices if by_pieces else 0
    ring = [(g, (g + 1) % groups) for g in range(groups)]
    own, sines, modes, total = setup(orbitals, table, mine)
    early = [total] * orbs
    for step in range(1, groups):
        last = step == groups - 1
        held = [lax.ppermute(h, "grp", ring) for h in held]
        for q in range(orbs):
            held[q], _ = lax.optimization_barrier((held[q], early[q]))
        early = []
        for tasks in [(True, False)] if last else [(True,), (False,)]:
            name = f"pairs_{step}_{len(early)}"
            total = pair_step(name, n, slots, pieces, tasks, last, mine, own, sines, modes, held, total)
            early.insert(0, total)
        early = early[-1:] * (orbs - 1) + [early[0]]
    if not pieces:
        whole = total.reshape(orbs, n * plane)
        return lax.all_to_all(whole, "dev", split_axis=1, concat_axis=0, tiled=True).astype(f32)
    arrived = [total[0]]
    for k in range(1, devices):
        arrived.append(lax.ppermute(total[k], "dev", [(d, d ^ k) for d in range(devices)]))
    return pl.pallas_call(
        functools.partial(gather_kernel, n, orbs),
        out_shape=jax.ShapeDtypeStruct((orbs * devices, n * plane // devices), f32),
        in_specs=[smem] + [vmem] * devices,
        out_specs=vmem,
        scratch_shapes=[pltpu.VMEM((orbs * n * plane // LANES, LANES), f32)] * 2,
        compiler_params=pltpu.CompilerParams(vmem_limit_bytes=32 << 20),
        name="cells",
    )(member.reshape(1), *arrived)


def solution(mesh):
    return jax.shard_map(
        body,
        mesh=mesh,
        in_specs=(
            P(("grp", "dev"), None, None),
            P(("grp", "dev"), None),
            P("grp", None, None),
            P("grp", "dev", None),
            P("grp", "dev", None),
            P("grp", "dev", None),
        ),
        out_specs=P("grp", "dev"),
        check_vma=False,
    )
```

profile of v0, /device:TPU:0, one launch (start us, length us, event | category | flops | bytes accessed | tf_op | source)
XLA Modules:
  0.0 52.0 jit_solution(11764110663468225015)
XLA Ops:
  0.0 1.0 %slice_bitcast_fusion = bf16[48,2304]{1,0:T(8,128)(2,1)S(1)} fusion(bf16[2,48,2304]{2,1,0:T(8,128)(2,1)} %own.1), kind=kLoop, calls=%fused_computation | loop fusion | bytes 442368 | tf_op jit(solution)/shard_map/squeeze | solution.py:401
  1.0 3.1 %collective-permute-start = (bf16[48,2304]{1,0:T(8,128)(2,1)S(1)}, bf16[48,2304]{1,0:T(8,128)(2,1)S(1)}, u32[]{:S(2)}, u32[]{:S(2)}) collective-permute-start(bf16[48,2304]{1,0:T(8,128)(2,1)S(1)} %slice_bitcast_fusion), channel_id=1, source_target_pairs={{0,8},{8,16},{16,24},{24,0},{1,9},{9,17},{17,25},{25,1},{2,10},{10... | collective-permute-start | bytes 663560 | tf_op jit(solution)/shard_map/ppermute | solution.py:409
  4.8 1.7 %pack.1 = (bf16[16,7040]{1,0:T(8,128)(2,1)}, s32[1,17]{1,0:T(1,128)}) custom-call(s32[2,3]{1,0:T(2,128)} %offsets.1, s32[1,4,8]{2,1,0:T(4,128)} %bitcast.4, s32[1,1,2]{2,1,0:T(1,128)} %pair_local.1, s32[1,1,2]{2,1,0:T(1,128)} %pair_source.1, s32[1,1,1]{2,1,0:T(1,128)S(6)} %copy.16.pair_count, bf16[2,48,2304]{2,1,0:T(8,128)(2,1)} %own.1), custom_call_target="tpu_custom_call" | custom-call | tf_op jit(solution)/shard_map/pack/pallas_call | solution.py:390
  6.5 1.6 %collective-permute-start.2 = (bf16[16,7040]{1,0:T(8,128)(2,1)}, bf16[16,7040]{1,0:T(8,128)(2,1)S(1)}, u32[]{:S(2)}, u32[]{:S(2)}) collective-permute-start(bf16[16,7040]{1,0:T(8,128)(2,1)} %get-tuple-element.31), channel_id=1, source_target_pairs={{0,8},{8,16},{16,24},{24,0},{1,9},{9,17},{17,25},{25,1},{2,10},{10... | collective-permute-start | bytes 675848 | tf_op jit(solution)/shard_map/ppermute | solution.py:409
  8.1 1.0 %copy-done.1 = f32[304,384]{1,0:T(8,128)S(1)} copy-done((f32[304,384]{1,0:T(8,128)S(1)}, f32[304,384]{1,0:T(8,128)}, u32[]{:S(2)}) %copy-start.1) | copy-done | bytes 466968
  9.1 0.7 %copy-done.2 = s32[1,17]{1,0:T(1,128)S(1)} copy-done((s32[1,17]{1,0:T(1,128)S(1)}, s32[1,17]{1,0:T(1,128)}, u32[]{:S(2)}) %copy-start.2) | copy-done | bytes 92
  9.8 0.9 %setup.1 = (f32[4608,128]{1,0:T(8,128)S(1)}, bf16[304,256]{1,0:T(8,128)(2,1)S(1)}, f32[72,128]{1,0:T(8,128)S(1)}, f32[2304,128]{1,0:T(8,128)S(1)}) custom-call(bf16[2,48,2304]{2,1,0:T(8,128)(2,1)S(1)} %copy-done, f32[304,384]{1,0:T(8,128)S(1)} %copy-done.1, s32[1,17]{1,0:T(1,128)S(1)} %copy-done.2), custom_call_target="tpu_custom_call" | custom-call | tf_op jit(solution)/shard_map/setup/pallas_call | solution.py:303
  10.7 1.7 %collective-permute-done.refs_4_ = bf16[48,2304]{1,0:T(8,128)(2,1)S(1)} collective-permute-done((bf16[48,2304]{1,0:T(8,128)(2,1)S(1)}, bf16[48,2304]{1,0:T(8,128)(2,1)S(1)}, u32[]{:S(2)}, u32[]{:S(2)}) %collective-permute-start) | collective-permute-done | bytes 221216 | tf_op jit(solution)/shard_map/ppermute | solution.py:409
  12.4 0.0 collective-permute-start.1
  12.4 4.8 %collective-permute-done.2.refs_5_ = bf16[16,7040]{1,0:T(8,128)(2,1)S(1)} collective-permute-done((bf16[16,7040]{1,0:T(8,128)(2,1)}, bf16[16,7040]{1,0:T(8,128)(2,1)S(1)}, u32[]{:S(2)}, u32[]{:S(2)}) %collective-permute-start.2) | collective-permute-done | bytes 225312 | tf_op jit(solution)/shard_map/ppermute | solution.py:409
  17.2 0.0 collective-permute-start.4
  17.2 0.7 %copy-done.3 = s32[1,17]{1,0:T(1,128)S(1)} copy-done((s32[1,17]{1,0:T(1,128)S(1)}, s32[1,17]{1,0:T(1,128)}, u32[]{:S(2)}) %copy-start.3) | copy-done | bytes 92
  17.9 2.8 %pairs_1_0.1.refs_6_ = f32[2304,128]{1,0:T(8,128)S(1)} custom-call(s32[1,17]{1,0:T(1,128)S(1)} %copy-done.3, f32[4608,128]{1,0:T(8,128)S(1)} %get-tuple-element.26.refs_1_, bf16[304,256]{1,0:T(8,128)(2,1)S(1)} %get-tuple-element.27.refs_2_, f32[72,128]{1,0:T(8,128)S(1)} %get-tuple-element.28.refs_3_, ...), custom_call_target="tpu_custom_call", output_to_operand_aliasing={{}: (6, {})} | custom-call | flops 382205952 | bytes 1769472 | tf_op jit(solution)/shard_map/pairs_1_0/pallas_call | solution.py:342
  20.7 1.4 %collective-permute-done.1.refs_4_ = bf16[48,2304]{1,0:T(8,128)(2,1)S(1)} collective-permute-done((bf16[48,2304]{1,0:T(8,128)(2,1)S(1)}, bf16[48,2304]{1,0:T(8,128)(2,1)S(1)}, u32[]{:S(2)}, u32[]{:S(2)}) %collective-permute-start.1) | collective-permute-done | bytes 221216 | tf_op jit(solution)/shard_map/ppermute | solution.py:409
  22.1 2.9 %pairs_1_1.1.refs_6_ = f32[2304,128]{1,0:T(8,128)S(1)} custom-call(s32[1,17]{1,0:T(1,128)S(1)} %copy-done.3, f32[4608,128]{1,0:T(8,128)S(1)} %get-tuple-element.26.refs_1_, bf16[304,256]{1,0:T(8,128)(2,1)S(1)} %get-tuple-element.27.refs_2_, f32[72,128]{1,0:T(8,128)S(1)} %get-tuple-element.28.refs_3_, ...), custom_call_target="tpu_custom_call", output_to_operand_aliasing={{}: (6, {})} | custom-call | flops 382205952 | bytes 1769472 | tf_op jit(solution)/shard_map/pairs_1_1/pallas_call | solution.py:342
  25.0 2.5 %collective-permute-done.4.refs_5_ = bf16[16,7040]{1,0:T(8,128)(2,1)S(1)} collective-permute-done((bf16[16,7040]{1,0:T(8,128)(2,1)S(1)}, bf16[16,7040]{1,0:T(8,128)(2,1)S(1)}, u32[]{:S(2)}, u32[]{:S(2)}) %collective-permute-start.4) | collective-permute-done | bytes 225312 | tf_op jit(solution)/shard_map/ppermute | solution.py:409
  27.5 0.8 %pairs_2_0.1.refs_6_ = f32[2304,128]{1,0:T(8,128)S(1)} custom-call(s32[1,17]{1,0:T(1,128)S(1)} %copy-done.3, f32[4608,128]{1,0:T(8,128)S(1)} %get-tuple-element.26.refs_1_, bf16[304,256]{1,0:T(8,128)(2,1)S(1)} %get-tuple-element.27.refs_2_, f32[72,128]{1,0:T(8,128)S(1)} %get-tuple-element.28.refs_3_, ...), custom_call_target="tpu_custom_call", output_to_operand_aliasing={{}: (6, {})} | custom-call | flops 382205952 | bytes 1769472 | tf_op jit(solution)/shard_map/pairs_2_0/pallas_call | solution.py:342
  28.3 4.0 %collective-permute-done.3.refs_4_ = bf16[48,2304]{1,0:T(8,128)(2,1)S(1)} collective-permute-done((bf16[48,2304]{1,0:T(8,128)(2,1)S(1)}, bf16[48,2304]{1,0:T(8,128)(2,1)S(1)}, u32[]{:S(2)}, u32[]{:S(2)}) %collective-permute-start.3) | collective-permute-done | bytes 221216 | tf_op jit(solution)/shard_map/ppermute | solution.py:409
  32.3 0.8 %pairs_2_1.1.refs_6_ = f32[2304,128]{1,0:T(8,128)S(1)} custom-call(s32[1,17]{1,0:T(1,128)S(1)} %copy-done.3, f32[4608,128]{1,0:T(8,128)S(1)} %get-tuple-element.26.refs_1_, bf16[304,256]{1,0:T(8,128)(2,1)S(1)} %get-tuple-element.27.refs_2_, f32[72,128]{1,0:T(8,128)S(1)} %get-tuple-element.28.refs_3_, ...), custom_call_target="tpu_custom_call", output_to_operand_aliasing={{}: (6, {})} | custom-call | flops 382205952 | bytes 1769472 | tf_op jit(solution)/shard_map/pairs_2_1/pallas_call | solution.py:342
  33.1 2.4 %collective-permute-done.5.refs_5_ = bf16[16,7040]{1,0:T(8,128)(2,1)S(1)} collective-permute-done((bf16[16,7040]{1,0:T(8,128)(2,1)S(1)}, bf16[16,7040]{1,0:T(8,128)(2,1)S(1)}, u32[]{:S(2)}, u32[]{:S(2)}) %collective-permute-start.5) | collective-permute-done | bytes 225312 | tf_op jit(solution)/shard_map/ppermute | solution.py:409
  35.5 5.5 %pairs_3_0.1 = (bf16[8,3456]{1,0:T(8,128)(2,1)S(1)}, bf16[8,3456]{1,0:T(8,128)(2,1)S(1)}, bf16[8,3456]{1,0:T(8,128)(2,1)S(1)}, bf16[8,3456]{1,0:T(8,128)(2,1)S(1...) custom-call(s32[1,17]{1,0:T(1,128)S(1)} %copy-done.3, ...), custom_call_target="tpu_custom_call" | custom-call | flops 382205952 | bytes 1769472 | tf_op jit(solution)/shard_map/pairs_3_0/pallas_call | solution.py:342
  41.0 0.1 collective-permute-start.10
  41.1 2.5 %collective-permute-start.11 = (bf16[8,3456]{1,0:T(8,128)(2,1)S(1)}, bf16[8,3456]{1,0:T(8,128)(2,1)S(1)}, u32[]{:S(2)}, u32[]{:S(2)}) collective-permute-start(bf16[8,3456]{1,0:T(8,128)(2,1)S(1)} %get-tuple-element.43), channel_id=1, source_target_pairs={{0,6},{1,7},{2,4},{3,5},{4,2},{5,3},{6,0},{7,1},{8,14},{9,15},{10,... | collective-permute-start | bytes 165896 | tf_op jit(solution)/shard_map/ppermute | solution.py:423
  43.6 0.6 %collective-permute-start.6 = (bf16[8,3456]{1,0:T(8,128)(2,1)S(1)}, bf16[8,3456]{1,0:T(8,128)(2,1)S(1)}, u32[]{:S(2)}, u32[]{:S(2)}) collective-permute-start(bf16[8,3456]{1,0:T(8,128)(2,1)S(1)} %get-tuple-element.38), channel_id=1, source_target_pairs={{0,1},{1,0},{2,3},{3,2},{4,5},{5,4},{6,7},{7,6},{8,9},{9,8},{10,11... | collective-permute-start | bytes 165896 | tf_op jit(solution)/shard_map/ppermute | solution.py:423
  44.2 2.2 %collective-permute-start.7 = (bf16[8,3456]{1,0:T(8,128)(2,1)S(1)}, bf16[8,3456]{1,0:T(8,128)(2,1)S(1)}, u32[]{:S(2)}, u32[]{:S(2)}) collective-permute-start(bf16[8,3456]{1,0:T(8,128)(2,1)S(1)} %get-tuple-element.39), channel_id=1, source_target_pairs={{0,2},{1,3},{2,0},{3,1},{4,6},{5,7},{6,4},{7,5},{8,10},{9,11},{10,... | collective-permute-start | bytes 165896 | tf_op jit(solution)/shard_map/ppermute | solution.py:423
  46.4 0.1 collective-permute-start.8
  46.6 0.7 %collective-permute-start.9 = (bf16[8,3456]{1,0:T(8,128)(2,1)S(1)}, bf16[8,3456]{1,0:T(8,128)(2,1)S(1)}, u32[]{:S(2)}, u32[]{:S(2)}) collective-permute-start(bf16[8,3456]{1,0:T(8,128)(2,1)S(1)} %get-tuple-element.41), channel_id=1, source_target_pairs={{0,4},{1,5},{2,6},{3,7},{4,0},{5,1},{6,2},{7,3},{8,12},{9,13},{10,... | collective-permute-start | bytes 165896 | tf_op jit(solution)/shard_map/ppermute | solution.py:423
  47.3 0.7 %collective-permute-done.12.refs_7_ = bf16[8,3456]{1,0:T(8,128)(2,1)S(1)} collective-permute-done((bf16[8,3456]{1,0:T(8,128)(2,1)S(1)}, bf16[8,3456]{1,0:T(8,128)(2,1)S(1)}, u32[]{:S(2)}, u32[]{:S(2)}) %collective-permute-start.12) | collective-permute-done | bytes 55328 | tf_op jit(solution)/shard_map/ppermute | solution.py:423
  48.1 1.6 %collective-permute-done.7.refs_2_ = bf16[8,3456]{1,0:T(8,128)(2,1)S(1)} collective-permute-done((bf16[8,3456]{1,0:T(8,128)(2,1)S(1)}, bf16[8,3456]{1,0:T(8,128)(2,1)S(1)}, u32[]{:S(2)}, u32[]{:S(2)}) %collective-permute-start.7) | collective-permute-done | bytes 55328 | tf_op jit(solution)/shard_map/ppermute | solution.py:423
  49.6 0.8 %collective-permute-done.8.refs_3_ = bf16[8,3456]{1,0:T(8,128)(2,1)S(1)} collective-permute-done((bf16[8,3456]{1,0:T(8,128)(2,1)S(1)}, bf16[8,3456]{1,0:T(8,128)(2,1)S(1)}, u32[]{:S(2)}, u32[]{:S(2)}) %collective-permute-start.8) | collective-permute-done | bytes 55328 | tf_op jit(solution)/shard_map/ppermute | solution.py:423
  50.5 0.3 collective-permute-done.9.refs_4_
  50.7 1.3 %cells.1 = f32[16,13824]{1,0:T(8,128)} custom-call(s32[1]{0:T(128)} %bitcast.member_ref, bf16[8,3456]{1,0:T(8,128)(2,1)S(1)} %get-tuple-element.37.refs_0_, bf16[8,3456]{1,0:T(8,128)(2,1)S(1)} %collective-permute-done.6.refs_1_, bf16[8,3456]{1,0:T(8,128)(2,1)S(1)} %collective-permute-done.7.refs_2_, bf16[8,3456]{1,0:T(8,128)(2,1)S(1)} %collective-permute-done.8.refs_3_, ...), custom_call_target="tpu_custom_call" | custom-call | tf_op jit(solution)/shard_map/cells/pallas_call | solution.py:424
  (11 shorter events, 0.0 us)
Async XLA Ops:
  0.0 8.1 %copy-start = (bf16[2,48,2304]{2,1,0:T(8,128)(2,1)S(1)}, bf16[2,48,2304]{2,1,0:T(8,128)(2,1)}, u32[]{:S(2)}) copy-start(bf16[2,48,2304]{2,1,0:T(8,128)(2,1)} %own.1) | copy-start | bytes 1327108
  1.0 11.4 %collective-permute-start = (bf16[48,2304]{1,0:T(8,128)(2,1)S(1)}, bf16[48,2304]{1,0:T(8,128)(2,1)S(1)}, u32[]{:S(2)}, u32[]{:S(2)}) collective-permute-start(bf16[48,2304]{1,0:T(8,128)(2,1)S(1)} %slice_bitcast_fusion), channel_id=1, source_target_pairs={{0,8},{8,16},{16,24},{24,0},{1,9},{9,17},{17,25},{25,1},{2,10},{10... | collective-permute-start | bytes 663560 | tf_op jit(solution)/shard_map/ppermute | solution.py:409
  6.5 10.8 %collective-permute-start.2 = (bf16[16,7040]{1,0:T(8,128)(2,1)}, bf16[16,7040]{1,0:T(8,128)(2,1)S(1)}, u32[]{:S(2)}, u32[]{:S(2)}) collective-permute-start(bf16[16,7040]{1,0:T(8,128)(2,1)} %get-tuple-element.31), channel_id=1, source_target_pairs={{0,8},{8,16},{16,24},{24,0},{1,9},{9,17},{17,25},{25,1},{2,10},{10... | collective-permute-start | bytes 675848 | tf_op jit(solution)/shard_map/ppermute | solution.py:409
  8.1 1.0 %copy-start.1 = (f32[304,384]{1,0:T(8,128)S(1)}, f32[304,384]{1,0:T(8,128)}, u32[]{:S(2)}) copy-start(f32[304,384]{1,0:T(8,128)} %constant.6.clone.table) | copy-start | bytes 1400836
  9.1 0.7 %copy-start.2 = (s32[1,17]{1,0:T(1,128)S(1)}, s32[1,17]{1,0:T(1,128)}, u32[]{:S(2)}) copy-start(s32[1,17]{1,0:T(1,128)} %get-tuple-element.25.mine.refs_0_) | copy-start | bytes 208
  12.4 9.7 %collective-permute-start.1 = (bf16[48,2304]{1,0:T(8,128)(2,1)S(1)}, bf16[48,2304]{1,0:T(8,128)(2,1)S(1)}, u32[]{:S(2)}, u32[]{:S(2)}) collective-permute-start(bf16[48,2304]{1,0:T(8,128)(2,1)S(1)} %collective-permute-done.refs_4_), channel_id=1, source_target_pairs={{0,8},{8,16},{16,24},{24,0},{1,9},{9,17},{17,25},{25,1},{2,10},{10... | collective-permute-start | bytes 663560 | tf_op jit(solution)/shard_map/ppermute | solution.py:409
  17.2 10.3 %collective-permute-start.4 = (bf16[16,7040]{1,0:T(8,128)(2,1)S(1)}, bf16[16,7040]{1,0:T(8,128)(2,1)S(1)}, u32[]{:S(2)}, u32[]{:S(2)}) collective-permute-start(bf16[16,7040]{1,0:T(8,128)(2,1)S(1)} %collective-permute-done.2.refs_5_), channel_id=1, source_target_pairs={{0,8},{8,16},{16,24},{24,0},{1,9},{9,17},{17,25},{25,1},{2,10},{10... | collective-permute-start | bytes 675848 | tf_op jit(solution)/shard_map/ppermute | solution.py:409
  17.2 0.7 %copy-start.3 = (s32[1,17]{1,0:T(1,128)S(1)}, s32[1,17]{1,0:T(1,128)}, u32[]{:S(2)}) copy-start(s32[1,17]{1,0:T(1,128)} %get-tuple-element.25.mine.refs_0_) | copy-start | bytes 208
  22.1 10.2 %collective-permute-start.3 = (bf16[48,2304]{1,0:T(8,128)(2,1)S(1)}, bf16[48,2304]{1,0:T(8,128)(2,1)S(1)}, u32[]{:S(2)}, u32[]{:S(2)}) collective-permute-start(bf16[48,2304]{1,0:T(8,128)(2,1)S(1)} %collective-permute-done.1.refs_4_), channel_id=1, source_target_pairs={{0,8},{8,16},{16,24},{24,0},{1,9},{9,17},{17,25},{25,1},{2,10},{10... | collective-permute-start | bytes 663560 | tf_op jit(solution)/shard_map/ppermute | solution.py:409
  27.5 8.1 %collective-permute-start.5 = (bf16[16,7040]{1,0:T(8,128)(2,1)S(1)}, bf16[16,7040]{1,0:T(8,128)(2,1)S(1)}, u32[]{:S(2)}, u32[]{:S(2)}) collective-permute-start(bf16[16,7040]{1,0:T(8,128)(2,1)S(1)} %collective-permute-done.4.refs_5_), channel_id=1, source_target_pairs={{0,8},{8,16},{16,24},{24,0},{1,9},{9,17},{17,25},{25,1},{2,10},{10... | collective-permute-start | bytes 675848 | tf_op jit(solution)/shard_map/ppermute | solution.py:409
  41.0 5.4 %collective-permute-start.10 = (bf16[8,3456]{1,0:T(8,128)(2,1)S(1)}, bf16[8,3456]{1,0:T(8,128)(2,1)S(1)}, u32[]{:S(2)}, u32[]{:S(2)}) collective-permute-start(bf16[8,3456]{1,0:T(8,128)(2,1)S(1)} %get-tuple-element.42), channel_id=1, source_target_pairs={{0,5},{1,4},{2,7},{3,6},{4,1},{5,0},{6,3},{7,2},{8,13},{9,12},{10,... | collective-permute-start | bytes 165896 | tf_op jit(solution)/shard_map/ppermute | solution.py:423
  41.1 5.5 %collective-permute-start.11 = (bf16[8,3456]{1,0:T(8,128)(2,1)S(1)}, bf16[8,3456]{1,0:T(8,128)(2,1)S(1)}, u32[]{:S(2)}, u32[]{:S(2)}) collective-permute-start(bf16[8,3456]{1,0:T(8,128)(2,1)S(1)} %get-tuple-element.43), channel_id=1, source_target_pairs={{0,6},{1,7},{2,4},{3,5},{4,2},{5,3},{6,0},{7,1},{8,14},{9,15},{10,... | collective-permute-start | bytes 165896 | tf_op jit(solution)/shard_map/ppermute | solution.py:423
  43.6 4.5 %collective-permute-start.12 = (bf16[8,3456]{1,0:T(8,128)(2,1)S(1)}, bf16[8,3456]{1,0:T(8,128)(2,1)S(1)}, u32[]{:S(2)}, u32[]{:S(2)}) collective-permute-start(bf16[8,3456]{1,0:T(8,128)(2,1)S(1)} %get-tuple-element.44), channel_id=1, source_target_pairs={{0,7},{1,6},{2,5},{3,4},{4,3},{5,2},{6,1},{7,0},{8,15},{9,14},{10,... | collective-permute-start | bytes 165896 | tf_op jit(solution)/shard_map/ppermute | solution.py:423
  43.6 4.5 %collective-permute-start.6 = (bf16[8,3456]{1,0:T(8,128)(2,1)S(1)}, bf16[8,3456]{1,0:T(8,128)(2,1)S(1)}, u32[]{:S(2)}, u32[]{:S(2)}) collective-permute-start(bf16[8,3456]{1,0:T(8,128)(2,1)S(1)} %get-tuple-element.38), channel_id=1, source_target_pairs={{0,1},{1,0},{2,3},{3,2},{4,5},{5,4},{6,7},{7,6},{8,9},{9,8},{10,11... | collective-permute-start | bytes 165896 | tf_op jit(solution)/shard_map/ppermute | solution.py:423
  44.2 5.5 %collective-permute-start.7 = (bf16[8,3456]{1,0:T(8,128)(2,1)S(1)}, bf16[8,3456]{1,0:T(8,128)(2,1)S(1)}, u32[]{:S(2)}, u32[]{:S(2)}) collective-permute-start(bf16[8,3456]{1,0:T(8,128)(2,1)S(1)} %get-tuple-element.39), channel_id=1, source_target_pairs={{0,2},{1,3},{2,0},{3,1},{4,6},{5,7},{6,4},{7,5},{8,10},{9,11},{10,... | collective-permute-start | bytes 165896 | tf_op jit(solution)/shard_map/ppermute | solution.py:423
  46.4 4.0 %collective-permute-start.8 = (bf16[8,3456]{1,0:T(8,128)(2,1)S(1)}, bf16[8,3456]{1,0:T(8,128)(2,1)S(1)}, u32[]{:S(2)}, u32[]{:S(2)}) collective-permute-start(bf16[8,3456]{1,0:T(8,128)(2,1)S(1)} %get-tuple-element.40), channel_id=1, source_target_pairs={{0,3},{1,2},{2,1},{3,0},{4,7},{5,6},{6,5},{7,4},{8,11},{9,10},{10,... | collective-permute-start | bytes 165896 | tf_op jit(solution)/shard_map/ppermute | solution.py:423
  46.6 4.2 %collective-permute-start.9 = (bf16[8,3456]{1,0:T(8,128)(2,1)S(1)}, bf16[8,3456]{1,0:T(8,128)(2,1)S(1)}, u32[]{:S(2)}, u32[]{:S(2)}) collective-permute-start(bf16[8,3456]{1,0:T(8,128)(2,1)S(1)} %get-tuple-element.41), channel_id=1, source_target_pairs={{0,4},{1,5},{2,6},{3,7},{4,0},{5,1},{6,2},{7,3},{8,12},{9,13},{10,... | collective-permute-start | bytes 165896 | tf_op jit(solution)/shard_map/ppermute | solution.py:423
where the time goes:
time: 52.3 us; the launch traced here: 52 us
  waiting for transfers between devices  20.2 us (39%)
  Pallas kernels  16.7 us (32%)
  starting transfers between devices  11 us (21%)
  local copies, waits for them, and re-layouts  3.4 us (7%)
  between operations  0.73 us (1%)
    ppermute x6, waiting for transfers between devices, body(): held = [lax.ppermute(h, 'grp', ring) for h in held]  16.7 us
    pallas_call x5, Pallas kernels, pair_step(): pl.pallas_call(functools.partial(pair_kernel, (n, orbs, slots), pieces, t...  12.8 us
    ppermute x7, starting transfers between devices, body(): lax.ppermute(total[k], 'dev', [(d, d ^ k) for d in range(devices)])  6.31 us
    ppermute x6, starting transfers between devices, body(): held = [lax.ppermute(h, 'grp', ring) for h in held]  4.72 us
    ppermute x7, waiting for transfers between devices, body(): lax.ppermute(total[k], 'dev', [(d, d ^ k) for d in range(devices)])  3.42 us
    unnamed x8, local copies, waits for them, and re-layouts  2.37 us
    pallas_call x1, Pallas kernels, body(): pl.pallas_call(functools.partial(pack_kernel, groups), grid=(1,), out_sha...  1.69 us
    pallas_call x1, Pallas kernels, body(): pl.pallas_call(functools.partial(gather_kernel, n, orbs), out_shape=jax.S...  1.3 us
  transfers between devices with their start and end apart: 13, of which 10 were waited for; matrix products, arithmetic and copies ran while one was open for 0% of the time, Pallas kernels for 19%

commit v1 on v0

--- a/solution.py
+++ b/solution.py
@@ -410,7 +410,7 @@
         for q in range(orbs):
             held[q], _ = lax.optimization_barrier((held[q], early[q]))
         early = []
-        for tasks in [(True, False)] if last else [(True,), (False,)]:
+        for tasks in [(True, False)] if step >= groups - 2 else [(True,), (False,)]:
             name = f"pairs_{step}_{len(early)}"
             total = pair_step(name, n, slots, pieces, tasks, last, mine, own, sines, modes, held, total)
             early.insert(0, total)

time: 52.3 us -> 55.4 us (1.059)
  waiting for transfers between devices: 20.2 us -> 24.2 us
  Pallas kernels: 16.7 us -> 13.9 us
  starting transfers between devices: 11 us -> 13 us
    ppermute x6, waiting for transfers between devices: 16.7 us -> 21.2 us  [body(): held = [lax.ppermute(h, 'grp', ring) for h in held]]
    pallas_call x5 -> x4, Pallas kernels: 12.8 us -> 9.98 us  [pair_step(): pl.pallas_call(functools.partial(pair_kernel, (n, orbs, slots), pieces, t...]
    ppermute x6, starting transfers between devices: 4.72 us -> 6 us  [body(): held = [lax.ppermute(h, 'grp', ring) for h in held]]
    ppermute x7, starting transfers between devices: 6.31 us -> 7.03 us  [body(): lax.ppermute(total[k], 'dev', [(d, d ^ k) for d in range(devices)])]
  transfers between devices with their start and end apart: 13 -> 13, of which waited for: 10 -> 9; matrix products, arithmetic and copies ran while one was open for 0% -> 0% of each run, Pallas kernels for 19% -> 13%
where the time goes in v1:
time: 55.4 us; the launch traced here: 55.2 us
  waiting for transfers between devices  24.2 us (44%)
  Pallas kernels  13.9 us (25%)
  starting transfers between devices  13 us (23%)
  local copies, waits for them, and re-layouts  3.4 us (6%)
  between operations  0.73 us (1%)
    ppermute x6, waiting for transfers between devices, body(): held = [lax.ppermute(h, 'grp', ring) for h in held]  21.2 us
    pallas_call x4, Pallas kernels, pair_step(): pl.pallas_call(functools.partial(pair_kernel, (n, orbs, slots), pieces, t...  9.98 us
    ppermute x7, starting transfers between devices, body(): lax.ppermute(total[k], 'dev', [(d, d ^ k) for d in range(devices)])  7.03 us
    ppermute x6, starting transfers between devices, body(): held = [lax.ppermute(h, 'grp', ring) for h in held]  6 us
    ppermute x7, waiting for transfers between devices, body(): lax.ppermute(total[k], 'dev', [(d, d ^ k) for d in range(devices)])  2.94 us
    unnamed x8, local copies, waits for them, and re-layouts  2.37 us
    pallas_call x1, Pallas kernels, body(): pl.pallas_call(functools.partial(pack_kernel, groups), grid=(1,), out_sha...  1.69 us
    pallas_call x1, Pallas kernels, body(): pl.pallas_call(functools.partial(gather_kernel, n, orbs), out_shape=jax.S...  1.3 us
  transfers between devices with their start and end apart: 13, of which 9 were waited for; matrix products, arithmetic and copies ran while one was open for 0% of the time, Pallas kernels for 13%

profile of v1, /device:TPU:0, one launch (start us, length us, event | category | flops | bytes accessed | tf_op | source)
XLA Modules:
  0.0 55.2 jit_solution(15945567376921599337)
XLA Ops:
  0.0 1.0 %slice_bitcast_fusion = bf16[48,2304]{1,0:T(8,128)(2,1)S(1)} fusion(bf16[2,48,2304]{2,1,0:T(8,128)(2,1)} %own.1), kind=kLoop, calls=%fused_computation | loop fusion | bytes 442368 | tf_op jit(solution)/shard_map/squeeze | solution.py:401
  1.0 3.1 %collective-permute-start = (bf16[48,2304]{1,0:T(8,128)(2,1)S(1)}, bf16[48,2304]{1,0:T(8,128)(2,1)S(1)}, u32[]{:S(2)}, u32[]{:S(2)}) collective-permute-start(bf16[48,2304]{1,0:T(8,128)(2,1)S(1)} %slice_bitcast_fusion), channel_id=1, source_target_pairs={{0,8},{8,16},{16,24},{24,0},{1,9},{9,17},{17,25},{25,1},{2,10},{10... | collective-permute-start | bytes 663560 | tf_op jit(solution)/shard_map/ppermute | solution.py:409
  4.8 1.7 %pack.1 = (bf16[16,7040]{1,0:T(8,128)(2,1)}, s32[1,17]{1,0:T(1,128)}) custom-call(s32[2,3]{1,0:T(2,128)} %offsets.1, s32[1,4,8]{2,1,0:T(4,128)} %bitcast.4, s32[1,1,2]{2,1,0:T(1,128)} %pair_local.1, s32[1,1,2]{2,1,0:T(1,128)} %pair_source.1, s32[1,1,1]{2,1,0:T(1,128)S(6)} %copy.14.pair_count, bf16[2,48,2304]{2,1,0:T(8,128)(2,1)} %own.1), custom_call_target="tpu_custom_call" | custom-call | tf_op jit(solution)/shard_map/pack/pallas_call | solution.py:390
  6.5 1.6 %collective-permute-start.2 = (bf16[16,7040]{1,0:T(8,128)(2,1)}, bf16[16,7040]{1,0:T(8,128)(2,1)S(1)}, u32[]{:S(2)}, u32[]{:S(2)}) collective-permute-start(bf16[16,7040]{1,0:T(8,128)(2,1)} %get-tuple-element.31), channel_id=1, source_target_pairs={{0,8},{8,16},{16,24},{24,0},{1,9},{9,17},{17,25},{25,1},{2,10},{10... | collective-permute-start | bytes 675848 | tf_op jit(solution)/shard_map/ppermute | solution.py:409
  8.1 1.0 %copy-done.1 = f32[304,384]{1,0:T(8,128)S(1)} copy-done((f32[304,384]{1,0:T(8,128)S(1)}, f32[304,384]{1,0:T(8,128)}, u32[]{:S(2)}) %copy-start.1) | copy-done | bytes 466968
  9.1 0.7 %copy-done.2 = s32[1,17]{1,0:T(1,128)S(1)} copy-done((s32[1,17]{1,0:T(1,128)S(1)}, s32[1,17]{1,0:T(1,128)}, u32[]{:S(2)}) %copy-start.2) | copy-done | bytes 92
  9.8 0.9 %setup.1 = (f32[4608,128]{1,0:T(8,128)S(1)}, bf16[304,256]{1,0:T(8,128)(2,1)S(1)}, f32[72,128]{1,0:T(8,128)S(1)}, f32[2304,128]{1,0:T(8,128)S(1)}) custom-call(bf16[2,48,2304]{2,1,0:T(8,128)(2,1)S(1)} %copy-done, f32[304,384]{1,0:T(8,128)S(1)} %copy-done.1, s32[1,17]{1,0:T(1,128)S(1)} %copy-done.2), custom_call_target="tpu_custom_call" | custom-call | tf_op jit(solution)/shard_map/setup/pallas_call | solution.py:303
  10.7 1.7 %collective-permute-done.refs_4_ = bf16[48,2304]{1,0:T(8,128)(2,1)S(1)} collective-permute-done((bf16[48,2304]{1,0:T(8,128)(2,1)S(1)}, bf16[48,2304]{1,0:T(8,128)(2,1)S(1)}, u32[]{:S(2)}, u32[]{:S(2)}) %collective-permute-start) | collective-permute-done | bytes 221216 | tf_op jit(solution)/shard_map/ppermute | solution.py:409
  12.4 4.8 %collective-permute-done.2.refs_5_ = bf16[16,7040]{1,0:T(8,128)(2,1)S(1)} collective-permute-done((bf16[16,7040]{1,0:T(8,128)(2,1)}, bf16[16,7040]{1,0:T(8,128)(2,1)S(1)}, u32[]{:S(2)}, u32[]{:S(2)}) %collective-permute-start.2) | collective-permute-done | bytes 225312 | tf_op jit(solution)/shard_map/ppermute | solution.py:409
  17.2 0.0 collective-permute-start.4
  17.2 0.7 %copy-done.3 = s32[1,17]{1,0:T(1,128)S(1)} copy-done((s32[1,17]{1,0:T(1,128)S(1)}, s32[1,17]{1,0:T(1,128)}, u32[]{:S(2)}) %copy-start.3) | copy-done | bytes 92
  17.9 0.8 %pairs_1_0.1.refs_6_ = f32[2304,128]{1,0:T(8,128)S(1)} custom-call(s32[1,17]{1,0:T(1,128)S(1)} %copy-done.3, f32[4608,128]{1,0:T(8,128)S(1)} %get-tuple-element.26.refs_1_, bf16[304,256]{1,0:T(8,128)(2,1)S(1)} %get-tuple-element.27.refs_2_, f32[72,128]{1,0:T(8,128)S(1)} %get-tuple-element.28.refs_3_, ...), custom_call_target="tpu_custom_call", output_to_operand_aliasing={{}: (6, {})} | custom-call | flops 382205952 | bytes 1769472 | tf_op jit(solution)/shard_map/pairs_1_0/pallas_call | solution.py:342
  18.7 3.4 %collective-permute-done.1.refs_4_ = bf16[48,2304]{1,0:T(8,128)(2,1)S(1)} collective-permute-done((bf16[48,2304]{1,0:T(8,128)(2,1)S(1)}, bf16[48,2304]{1,0:T(8,128)(2,1)S(1)}, u32[]{:S(2)}, u32[]{:S(2)}) %collective-permute-start.1) | collective-permute-done | bytes 221216 | tf_op jit(solution)/shard_map/ppermute | solution.py:409
  22.1 0.8 %pairs_1_1.1.refs_6_ = f32[2304,128]{1,0:T(8,128)S(1)} custom-call(s32[1,17]{1,0:T(1,128)S(1)} %copy-done.3, f32[4608,128]{1,0:T(8,128)S(1)} %get-tuple-element.26.refs_1_, bf16[304,256]{1,0:T(8,128)(2,1)S(1)} %get-tuple-element.27.refs_2_, f32[72,128]{1,0:T(8,128)S(1)} %get-tuple-element.28.refs_3_, ...), custom_call_target="tpu_custom_call", output_to_operand_aliasing={{}: (6, {})} | custom-call | flops 382205952 | bytes 1769472 | tf_op jit(solution)/shard_map/pairs_1_1/pallas_call | solution.py:342
  22.9 3.0 %collective-permute-done.4.refs_5_ = bf16[16,7040]{1,0:T(8,128)(2,1)S(1)} collective-permute-done((bf16[16,7040]{1,0:T(8,128)(2,1)S(1)}, bf16[16,7040]{1,0:T(8,128)(2,1)S(1)}, u32[]{:S(2)}, u32[]{:S(2)}) %collective-permute-start.4) | collective-permute-done | bytes 225312 | tf_op jit(solution)/shard_map/ppermute | solution.py:409
  26.0 0.0 collective-permute-start.5
  26.0 1.3 %collective-permute-start.3 = (bf16[48,2304]{1,0:T(8,128)(2,1)S(1)}, bf16[48,2304]{1,0:T(8,128)(2,1)S(1)}, u32[]{:S(2)}, u32[]{:S(2)}) collective-permute-start(bf16[48,2304]{1,0:T(8,128)(2,1)S(1)} %collective-permute-done.1.refs_4_), channel_id=1, source_target_pairs={{0,8},{8,16},{16,24},{24,0},{1,9},{9,17},{17,25},{25,1},{2,10},{10... | collective-permute-start | bytes 663560 | tf_op jit(solution)/shard_map/ppermute | solution.py:409
  27.2 2.9 %pairs_2_0.1.refs_6_ = f32[2304,128]{1,0:T(8,128)S(1)} custom-call(s32[1,17]{1,0:T(1,128)S(1)} %copy-done.3, f32[4608,128]{1,0:T(8,128)S(1)} %get-tuple-element.26.refs_1_, bf16[304,256]{1,0:T(8,128)(2,1)S(1)} %get-tuple-element.27.refs_2_, f32[72,128]{1,0:T(8,128)S(1)} %get-tuple-element.28.refs_3_, ...), custom_call_target="tpu_custom_call", output_to_operand_aliasing={{}: (6, {})} | custom-call | flops 382205952 | bytes 1769472 | tf_op jit(solution)/shard_map/pairs_2_0/pallas_call | solution.py:342
  30.2 8.3 %collective-permute-done.3.refs_4_ = bf16[48,2304]{1,0:T(8,128)(2,1)S(1)} collective-permute-done((bf16[48,2304]{1,0:T(8,128)(2,1)S(1)}, bf16[48,2304]{1,0:T(8,128)(2,1)S(1)}, u32[]{:S(2)}, u32[]{:S(2)}) %collective-permute-start.3) | collective-permute-done | bytes 221216 | tf_op jit(solution)/shard_map/ppermute | solution.py:409
  38.5 0.0 collective-permute-done.5.refs_5_
  38.5 5.4 %pairs_3_0.1 = (bf16[8,3456]{1,0:T(8,128)(2,1)S(1)}, bf16[8,3456]{1,0:T(8,128)(2,1)S(1)}, bf16[8,3456]{1,0:T(8,128)(2,1)S(1)}, bf16[8,3456]{1,0:T(8,128)(2,1)S(1...) custom-call(s32[1,17]{1,0:T(1,128)S(1)} %copy-done.3, ...), custom_call_target="tpu_custom_call" | custom-call | flops 382205952 | bytes 1769472 | tf_op jit(solution)/shard_map/pairs_3_0/pallas_call | solution.py:342
  44.0 0.1 collective-permute-start.10
  44.0 0.4 collective-permute-start.11
  44.5 3.4 %collective-permute-start.12 = (bf16[8,3456]{1,0:T(8,128)(2,1)S(1)}, bf16[8,3456]{1,0:T(8,128)(2,1)S(1)}, u32[]{:S(2)}, u32[]{:S(2)}) collective-permute-start(bf16[8,3456]{1,0:T(8,128)(2,1)S(1)} %get-tuple-element.44), channel_id=1, source_target_pairs={{0,7},{1,6},{2,5},{3,4},{4,3},{5,2},{6,1},{7,0},{8,15},{9,14},{10,... | collective-permute-start | bytes 165896 | tf_op jit(solution)/shard_map/ppermute | solution.py:423
  47.9 0.0 collective-permute-start.6
  47.9 0.2 collective-permute-done.10.refs_5_
  48.1 1.7 %collective-permute-start.8 = (bf16[8,3456]{1,0:T(8,128)(2,1)S(1)}, bf16[8,3456]{1,0:T(8,128)(2,1)S(1)}, u32[]{:S(2)}, u32[]{:S(2)}) collective-permute-start(bf16[8,3456]{1,0:T(8,128)(2,1)S(1)} %get-tuple-element.40), channel_id=1, source_target_pairs={{0,3},{1,2},{2,1},{3,0},{4,7},{5,6},{6,5},{7,4},{8,11},{9,10},{10,... | collective-permute-start | bytes 165896 | tf_op jit(solution)/shard_map/ppermute | solution.py:423
  49.8 1.4 %collective-permute-start.9 = (bf16[8,3456]{1,0:T(8,128)(2,1)S(1)}, bf16[8,3456]{1,0:T(8,128)(2,1)S(1)}, u32[]{:S(2)}, u32[]{:S(2)}) collective-permute-start(bf16[8,3456]{1,0:T(8,128)(2,1)S(1)} %get-tuple-element.41), channel_id=1, source_target_pairs={{0,4},{1,5},{2,6},{3,7},{4,0},{5,1},{6,2},{7,3},{8,12},{9,13},{10,... | collective-permute-start | bytes 165896 | tf_op jit(solution)/shard_map/ppermute | solution.py:423
  51.2 1.4 %collective-permute-done.7.refs_2_ = bf16[8,3456]{1,0:T(8,128)(2,1)S(1)} collective-permute-done((bf16[8,3456]{1,0:T(8,128)(2,1)S(1)}, bf16[8,3456]{1,0:T(8,128)(2,1)S(1)}, u32[]{:S(2)}, u32[]{:S(2)}) %collective-permute-start.7) | collective-permute-done | bytes 55328 | tf_op jit(solution)/shard_map/ppermute | solution.py:423
  52.6 0.4 collective-permute-done.8.refs_3_
  53.0 0.9 %collective-permute-done.9.refs_4_ = bf16[8,3456]{1,0:T(8,128)(2,1)S(1)} collective-permute-done((bf16[8,3456]{1,0:T(8,128)(2,1)S(1)}, bf16[8,3456]{1,0:T(8,128)(2,1)S(1)}, u32[]{:S(2)}, u32[]{:S(2)}) %collective-permute-start.9) | collective-permute-done | bytes 55328 | tf_op jit(solution)/shard_map/ppermute | solution.py:423
  54.0 1.3 %cells.1 = f32[16,13824]{1,0:T(8,128)} custom-call(s32[1]{0:T(128)} %bitcast.member_ref, bf16[8,3456]{1,0:T(8,128)(2,1)S(1)} %get-tuple-element.37.refs_0_, bf16[8,3456]{1,0:T(8,128)(2,1)S(1)} %collective-permute-done.6.refs_1_, bf16[8,3456]{1,0:T(8,128)(2,1)S(1)} %collective-permute-done.7.refs_2_, bf16[8,3456]{1,0:T(8,128)(2,1)S(1)} %collective-permute-done.8.refs_3_, ...), custom_call_target="tpu_custom_call" | custom-call | tf_op jit(solution)/shard_map/cells/pallas_call | solution.py:424
  (10 shorter events, 0.0 us)
Async XLA Ops:
  0.0 8.1 %copy-start = (bf16[2,48,2304]{2,1,0:T(8,128)(2,1)S(1)}, bf16[2,48,2304]{2,1,0:T(8,128)(2,1)}, u32[]{:S(2)}) copy-start(bf16[2,48,2304]{2,1,0:T(8,128)(2,1)} %own.1) | copy-start | bytes 1327108
  1.0 11.4 %collective-permute-start = (bf16[48,2304]{1,0:T(8,128)(2,1)S(1)}, bf16[48,2304]{1,0:T(8,128)(2,1)S(1)}, u32[]{:S(2)}, u32[]{:S(2)}) collective-permute-start(bf16[48,2304]{1,0:T(8,128)(2,1)S(1)} %slice_bitcast_fusion), channel_id=1, source_target_pairs={{0,8},{8,16},{16,24},{24,0},{1,9},{9,17},{17,25},{25,1},{2,10},{10... | collective-permute-start | bytes 663560 | tf_op jit(solution)/shard_map/ppermute | solution.py:409
  6.5 10.8 %collective-permute-start.2 = (bf16[16,7040]{1,0:T(8,128)(2,1)}, bf16[16,7040]{1,0:T(8,128)(2,1)S(1)}, u32[]{:S(2)}, u32[]{:S(2)}) collective-permute-start(bf16[16,7040]{1,0:T(8,128)(2,1)} %get-tuple-element.31), channel_id=1, source_target_pairs={{0,8},{8,16},{16,24},{24,0},{1,9},{9,17},{17,25},{25,1},{2,10},{10... | collective-permute-start | bytes 675848 | tf_op jit(solution)/shard_map/ppermute | solution.py:409
  8.1 1.0 %copy-start.1 = (f32[304,384]{1,0:T(8,128)S(1)}, f32[304,384]{1,0:T(8,128)}, u32[]{:S(2)}) copy-start(f32[304,384]{1,0:T(8,128)} %constant.6.clone.table) | copy-start | bytes 1400836
  9.1 0.7 %copy-start.2 = (s32[1,17]{1,0:T(1,128)S(1)}, s32[1,17]{1,0:T(1,128)}, u32[]{:S(2)}) copy-start(s32[1,17]{1,0:T(1,128)} %get-tuple-element.25.mine.refs_0_) | copy-start | bytes 208
  12.4 9.7 %collective-permute-start.1 = (bf16[48,2304]{1,0:T(8,128)(2,1)S(1)}, bf16[48,2304]{1,0:T(8,128)(2,1)S(1)}, u32[]{:S(2)}, u32[]{:S(2)}) collective-permute-start(bf16[48,2304]{1,0:T(8,128)(2,1)S(1)} %collective-permute-done.refs_4_), channel_id=1, source_target_pairs={{0,8},{8,16},{16,24},{24,0},{1,9},{9,17},{17,25},{25,1},{2,10},{10... | collective-permute-start | bytes 663560 | tf_op jit(solution)/shard_map/ppermute | solution.py:409
  17.2 8.7 %collective-permute-start.4 = (bf16[16,7040]{1,0:T(8,128)(2,1)S(1)}, bf16[16,7040]{1,0:T(8,128)(2,1)S(1)}, u32[]{:S(2)}, u32[]{:S(2)}) collective-permute-start(bf16[16,7040]{1,0:T(8,128)(2,1)S(1)} %collective-permute-done.2.refs_5_), channel_id=1, source_target_pairs={{0,8},{8,16},{16,24},{24,0},{1,9},{9,17},{17,25},{25,1},{2,10},{10... | collective-permute-start | bytes 675848 | tf_op jit(solution)/shard_map/ppermute | solution.py:409
  17.2 0.7 %copy-start.3 = (s32[1,17]{1,0:T(1,128)S(1)}, s32[1,17]{1,0:T(1,128)}, u32[]{:S(2)}) copy-start(s32[1,17]{1,0:T(1,128)} %get-tuple-element.25.mine.refs_0_) | copy-start | bytes 208
  26.0 12.6 %collective-permute-start.5 = (bf16[16,7040]{1,0:T(8,128)(2,1)S(1)}, bf16[16,7040]{1,0:T(8,128)(2,1)S(1)}, u32[]{:S(2)}, u32[]{:S(2)}) collective-permute-start(bf16[16,7040]{1,0:T(8,128)(2,1)S(1)} %collective-permute-done.4.refs_5_), channel_id=1, source_target_pairs={{0,8},{8,16},{16,24},{24,0},{1,9},{9,17},{17,25},{25,1},{2,10},{10... | collective-permute-start | bytes 675848 | tf_op jit(solution)/shard_map/ppermute | solution.py:409
  26.0 12.6 %collective-permute-start.3 = (bf16[48,2304]{1,0:T(8,128)(2,1)S(1)}, bf16[48,2304]{1,0:T(8,128)(2,1)S(1)}, u32[]{:S(2)}, u32[]{:S(2)}) collective-permute-start(bf16[48,2304]{1,0:T(8,128)(2,1)S(1)} %collective-permute-done.1.refs_4_), channel_id=1, source_target_pairs={{0,8},{8,16},{16,24},{24,0},{1,9},{9,17},{17,25},{25,1},{2,10},{10... | collective-permute-start | bytes 663560 | tf_op jit(solution)/shard_map/ppermute | solution.py:409
  44.0 4.2 %collective-permute-start.10 = (bf16[8,3456]{1,0:T(8,128)(2,1)S(1)}, bf16[8,3456]{1,0:T(8,128)(2,1)S(1)}, u32[]{:S(2)}, u32[]{:S(2)}) collective-permute-start(bf16[8,3456]{1,0:T(8,128)(2,1)S(1)} %get-tuple-element.42), channel_id=1, source_target_pairs={{0,5},{1,4},{2,7},{3,6},{4,1},{5,0},{6,3},{7,2},{8,13},{9,12},{10,... | collective-permute-start | bytes 165896 | tf_op jit(solution)/shard_map/ppermute | solution.py:423
  44.0 5.7 %collective-permute-start.11 = (bf16[8,3456]{1,0:T(8,128)(2,1)S(1)}, bf16[8,3456]{1,0:T(8,128)(2,1)S(1)}, u32[]{:S(2)}, u32[]{:S(2)}) collective-permute-start(bf16[8,3456]{1,0:T(8,128)(2,1)S(1)} %get-tuple-element.43), channel_id=1, source_target_pairs={{0,6},{1,7},{2,4},{3,5},{4,2},{5,3},{6,0},{7,1},{8,14},{9,15},{10,... | collective-permute-start | bytes 165896 | tf_op jit(solution)/shard_map/ppermute | solution.py:423
  44.5 6.7 %collective-permute-start.12 = (bf16[8,3456]{1,0:T(8,128)(2,1)S(1)}, bf16[8,3456]{1,0:T(8,128)(2,1)S(1)}, u32[]{:S(2)}, u32[]{:S(2)}) collective-permute-start(bf16[8,3456]{1,0:T(8,128)(2,1)S(1)} %get-tuple-element.44), channel_id=1, source_target_pairs={{0,7},{1,6},{2,5},{3,4},{4,3},{5,2},{6,1},{7,0},{8,15},{9,14},{10,... | collective-permute-start | bytes 165896 | tf_op jit(solution)/shard_map/ppermute | solution.py:423
  47.9 3.3 %collective-permute-start.6 = (bf16[8,3456]{1,0:T(8,128)(2,1)S(1)}, bf16[8,3456]{1,0:T(8,128)(2,1)S(1)}, u32[]{:S(2)}, u32[]{:S(2)}) collective-permute-start(bf16[8,3456]{1,0:T(8,128)(2,1)S(1)} %get-tuple-element.38), channel_id=1, source_target_pairs={{0,1},{1,0},{2,3},{3,2},{4,5},{5,4},{6,7},{7,6},{8,9},{9,8},{10,11... | collective-permute-start | bytes 165896 | tf_op jit(solution)/shard_map/ppermute | solution.py:423
  47.9 4.7 %collective-permute-start.7 = (bf16[8,3456]{1,0:T(8,128)(2,1)S(1)}, bf16[8,3456]{1,0:T(8,128)(2,1)S(1)}, u32[]{:S(2)}, u32[]{:S(2)}) collective-permute-start(bf16[8,3456]{1,0:T(8,128)(2,1)S(1)} %get-tuple-element.39), channel_id=1, source_target_pairs={{0,2},{1,3},{2,0},{3,1},{4,6},{5,7},{6,4},{7,5},{8,10},{9,11},{10,... | collective-permute-start | bytes 165896 | tf_op jit(solution)/shard_map/ppermute | solution.py:423
  48.1 4.9 %collective-permute-start.8 = (bf16[8,3456]{1,0:T(8,128)(2,1)S(1)}, bf16[8,3456]{1,0:T(8,128)(2,1)S(1)}, u32[]{:S(2)}, u32[]{:S(2)}) collective-permute-start(bf16[8,3456]{1,0:T(8,128)(2,1)S(1)} %get-tuple-element.40), channel_id=1, source_target_pairs={{0,3},{1,2},{2,1},{3,0},{4,7},{5,6},{6,5},{7,4},{8,11},{9,10},{10,... | collective-permute-start | bytes 165896 | tf_op jit(solution)/shard_map/ppermute | solution.py:423
  49.8 4.2 %collective-permute-start.9 = (bf16[8,3456]{1,0:T(8,128)(2,1)S(1)}, bf16[8,3456]{1,0:T(8,128)(2,1)S(1)}, u32[]{:S(2)}, u32[]{:S(2)}) collective-permute-start(bf16[8,3456]{1,0:T(8,128)(2,1)S(1)} %get-tuple-element.41), channel_id=1, source_target_pairs={{0,4},{1,5},{2,6},{3,7},{4,0},{5,1},{6,2},{7,3},{8,12},{9,13},{10,... | collective-permute-start | bytes 165896 | tf_op jit(solution)/shard_map/ppermute | solution.py:423
